TPU v7x, 512 devices: a whole 4x8x8 slice. The times are simulated.
512 devices in a mesh: bx: 32 (over x, y_lo, core), by: 16 (over z, y_hi).
Axes of the slice: x: 4, y: 8 (y_hi: 2, y_lo: 4; y = y_hi * 4 + y_lo), z: 8, core: 2. Of those that a mesh axis runs over, the one named last changes fastest.
Arguments:
- weights: float32 [2, 25, 128, 128, 128], P(None, None, 'bx', 'by'), may hold values from -6 to 6
Outputs:
- radon_data: float32 [8, 2, 32, 64], P(None, None, 'bx', 'by')
All inputs are finite; a program needn't handle non-finite values.
Results may differ from a plain program's by a relative error of at most 0.0013.
Values sent between devices are 32-bit elements; how exact they have to be, the bound alone decides.
A program may use at most 128 MiB of HBM per device.

v0:
```python
import functools
import math

import jax
import jax.numpy as jnp
import numpy as np
from jax import lax
from jax.experimental import pallas as pl
from jax.experimental.pallas import tpu as pltpu
from jax.sharding import PartitionSpec as P

N = 16384
P_SIZE = 5
LEVEL_BOXES = 128
EV = 8
NODES = P_SIZE * P_SIZE
ROWS = 2 * NODES
SLOT = 104
FIRST = 56
MESH = pl.DeviceIdType.MESH

SIN = (4.44288292, -7.3082457, 3.60635441, -0.84611289, 0.10982699)
COS = (1.4142135, -6.97885099, 5.73946117, -1.88356299, 0.31069819)


def nodes():
    return np.cos(np.pi * (2.0 * np.arange(P_SIZE) + 1.0) / (2.0 * P_SIZE)) / 2.0


def lower_table():
    z = nodes()
    child = -0.25 + z / 2.0
    table = np.ones((P_SIZE, P_SIZE))
    for m in range(P_SIZE):
        for j in range(P_SIZE):
            if j != m:
                table[m] *= (child - z[j]) / (z[m] - z[j])
    return table


Z = [float(v) for v in nodes()]
LOW = lower_table()
POINTS = [((f + 0.5) / EV - 0.5, ((3 * f) % EV + 0.5) / EV - 0.5) for f in range(EV)]


def turn(theta):
    u = theta - jnp.round(theta)
    w = u * u
    s = SIN[4]
    c = COS[4]
    for k in (3, 2, 1, 0):
        s = s * w + SIN[k]
        c = c * w + COS[k]
    s = s * u
    return 1.0 - s * s, s * c


def interpolate(low, high):
    even = [low[j] + high[4 - j] for j in range(5)]
    odd = [low[j] - high[4 - j] for j in range(5)]
    out = [None] * 5
    for m in (0, 1):
        a = sum_of(even, [0.5 * (LOW[m, j] + LOW[4 - m, j]) for j in range(5)])
        b = sum_of(odd, [0.5 * (LOW[m, j] - LOW[4 - m, j]) for j in range(5)])
        out[m] = a + b
        out[4 - m] = a - b
    out[2] = sum_of(even, [LOW[2, j] for j in range(5)])
    return out


def sum_of(values, factors):
    total = None
    for v, f in zip(values, factors):
        if abs(f) < 1e-14:
            continue
        term = v * float(f)
        total = term if total is None else total + term
    return total


def speeds(x1, x2):
    cp, _ = turn(x1 - x2)
    cq, _ = turn(x1 + x2)
    return (2.0 + 0.5 * (cp - cq)) * 0.0625, (2.0 + 0.5 * (cp + cq)) * 0.0625


def moved(x1, x2, c1, c2, d1, d2):
    dp, dq = d1 - d2, d1 + d2
    _, sp = turn(x1 - x2 + 0.5 * dp)
    _, sq = turn(x1 + x2 + 0.5 * dq)
    gp = sp * (-2.0 * math.sin(math.pi * dp))
    gq = sq * (-2.0 * math.sin(math.pi * dq))
    e1 = (gp - gq) * 0.03125
    e2 = (gp + gq) * 0.03125
    n1, n2 = c1 + e1, c2 + e2
    return n1 * n1, n2 * n2, e1 * (c1 + n1), e2 * (c2 + n2)


def root(s):
    return s * lax.rsqrt(s)


def inverse(s):
    return pltpu.reciprocal(s, approx=True)


def kernel(w_ref, o_ref, send, recv, st0, st1, tab, nrm, acc, part, final, send_sem, recv_sem, own_sem, fs_sem, fr_sem):
    bx, by = lax.axis_index("bx"), lax.axis_index("by")
    gi, gj = bx // 4, by // 4
    b0, b1 = bx % 2, (bx // 2) % 2
    c0, c1 = by % 2, (by // 2) % 2
    me = b0 + 2 * c0 + 4 * b1 + 8 * c1
    slot = gi * 4 + gj
    s_b1, s_c1, s_c0, s_b0 = gi // 4, (gi // 2) % 2, gi % 2, gj // 2
    source_x, source_y = s_b0 + 2 * s_b1, s_c0 + 2 * s_c1
    my_line, my_half = gj // 2, gj % 2
    is_self = (b0 == s_b0) & (b1 == s_b1) & (c0 == s_c0) & (c1 == s_c1)

    def peer(k):
        flip = lambda bit, at: (1 - bit) if (k >> at) & 1 else bit
        q0, r0, q1, r1 = flip(b0, 0), flip(c0, 1), flip(b1, 2), flip(c1, 3)
        return q0 + 2 * r0 + 4 * q1 + 8 * r1, (gi * 4 + q0 + 2 * q1, gj * 4 + r0 + 2 * r1)

    order = [k for k in range(16) if k & 2] + [k for k in range(1, 16) if not k & 2]

    barrier = pltpu.get_barrier_semaphore()
    for k in order:
        pl.semaphore_signal(barrier, inc=1, device_id=peer(k)[1], device_id_type=MESH)

    @pl.loop(0, 32)
    def _(g):
        @pl.when(jnp.logical_not(is_self & (g == slot)))
        def _():
            pl.semaphore_signal(
                barrier,
                inc=1,
                device_id=((g // 4) * 4 + source_x, (g % 4) * 4 + source_y),
                device_id_type=MESH,
            )

    lane = lax.broadcasted_iota(jnp.int32, (8, 128), 1)
    sub = lax.broadcasted_iota(jnp.int32, (8, 128), 0)
    bit = lambda v, at: (v >> at) & 1
    l6, l5, l4, l3 = (bit(lane, at) for at in (6, 5, 4, 3))
    s2, s1, s0 = (bit(sub, at) for at in (2, 1, 0))

    def shuffle(r):
        half, row = r // ROWS, r % ROWS
        x = [w_ref[row, 2 * half + q] for q in range(2)]
        y = [
            jnp.where(l5 == 0, x[0], pltpu.roll(x[1], 32, 1)),
            jnp.where(l5 == 0, pltpu.roll(x[0], 96, 1), x[1]),
        ]
        for h in range(2):
            v = y[h]
            v = jnp.where(s2 == l6, v, pltpu.roll(pltpu.roll(v, 4, 0), 64, 1))
            for s_bit, l_bit, by_sub, by_lane in ((s1, l4, 2, 16), (s0, l3, 1, 8)):
                up = pltpu.roll(pltpu.roll(v, 8 - by_sub, 0), by_lane, 1)
                down = pltpu.roll(pltpu.roll(v, by_sub, 0), 128 - by_lane, 1)
                v = jnp.where(s_bit == l_bit, v, jnp.where(s_bit == 0, up, down))
            send[pl.ds(h * 8 * SLOT + r, 8, stride=SLOT), :] = v

    def exchange(half, k):
        at, device = peer(k)
        start, count = ((0, FIRST), (FIRST, SLOT - FIRST))[half]
        return pltpu.make_async_remote_copy(
            src_ref=send.at[pl.ds(pl.multiple_of(at * SLOT + start, 8), count)],
            dst_ref=recv.at[pl.ds(pl.multiple_of(me * SLOT + start, 8), count)],
            send_sem=send_sem.at[half, k],
            recv_sem=recv_sem.at[half, k],
            device_id=device,
            device_id_type=MESH,
        )

    def own(half):
        start, count = ((0, FIRST), (FIRST, SLOT - FIRST))[half]
        rows = pl.ds(pl.multiple_of(me * SLOT + start, 8), count)
        return pltpu.make_async_copy(send.at[rows], recv.at[rows], own_sem.at[half])

    @pl.loop(0, FIRST // 4)
    def _(g):
        for u in range(4):
            shuffle(g * 4 + u)

    pl.semaphore_wait(barrier, 47 - is_self.astype(jnp.int32))
    for k in order:
        exchange(0, k).start()
    own(0).start()

    @pl.loop(FIRST // 4, NODES)
    def _(g):
        for u in range(4):
            shuffle(g * 4 + u)

    for k in order:
        exchange(1, k).start()
    own(1).start()

    f32 = lambda v: v.astype(jnp.float32)
    q_bit = l5
    box2 = 4 * l6 + 2 * l4 + l3
    line1 = 4 * b1 + 2 * c1 + c0
    line2 = 8 * b0 + (lane & 7)
    xa1 = (f32(jnp.zeros_like(lane) + ((17 * line1 + 3) % 128)) + 0.5) * (1.0 / 128)
    xa2 = (f32((29 * line2 + 11) & 127) + 0.5) * (1.0 / 128)
    m2, m1, m0 = f32(s2), f32(s1), f32(s0)
    h1, h2 = 1.0 / 256, 1.0 / 512

    def center(index, width):
        return f32(index) * width + (0.5 * width - N / 2.0)

    def split(level, p, load, dst):
        first = level == 0
        along = level % 2
        box1 = 2 * p + q_bit
        if level == 0:
            index = [lambda c: box1 * 32 + 4 * gi + 2 * s1 + c, lambda c: box2 * 16 + 4 * gj + 2 * s2 + s0]
            widths, x, step = (128.0, 128.0), (xa1, xa2), h1
        elif level == 1:
            index = [lambda c: box1 * 16 + 2 * gi + s0, lambda c: box2 * 16 + 4 * gj + 2 * s1 + c]
            widths, x, step = (256.0, 128.0), (xa1 + (m2 - 0.5) * h1, xa2), h1
        elif level == 2:
            index = [lambda c: box1 * 16 + 2 * gi + c, lambda c: box2 * 8 + 2 * gj + s0]
            widths, x, step = (256.0, 256.0), (xa1 + (m1 - 0.5) * h1, xa2 + (m2 - 0.5) * h1), h2
        else:
            index = [lambda c: box1 * 8 + gi, lambda c: box2 * 8 + 2 * gj + c]
            widths = (512.0, 256.0)
            x, step = (xa1 + (m0 - 0.5) * h1 + (m2 - 0.5) * h2, xa2 + (m1 - 0.5) * h1), h2
        speed = speeds(*x)
        base = (speed[0] * speed[0], speed[1] * speed[1])
        steps = ((e - 0.5) * step for e in range(2))
        new = []
        for s in steps:
            shift = (s, 0.0) if along == 0 else (0.0, s)
            new.append(moved(x[0], x[1], speed[0], speed[1], *shift) + (s,))
        other = 1 - along
        corner = []
        for c in range(2):
            mid = center(index[along](c), widths[along])
            for i in range(5):
                off = widths[along] * Z[i]
                k = mid + off
                sq = k * k
                if not first:
                    tab[0, c * 5 + i] = base[along] * sq
                for e in range(2):
                    a = new[e]
                    diff = a[2 + along] * sq
                    line = a[4] * k
                    if first:
                        diff += base[along] * (off * (k + mid))
                        line = a[4] * mid + (x[along] + a[4]) * off
                    tab[1 + 3 * e, c * 5 + i] = a[along] * sq
                    tab[2 + 3 * e, c * 5 + i] = diff
                    tab[3 + 3 * e, c * 5 + i] = line
            corner.append(base[along] * (mid * mid))
        mid = center(index[other](0), widths[other])
        for i in range(5):
            off = widths[other] * Z[i]
            k = mid + off
            sq = k * k
            tab[0, 10 + i] = x[other] * off if first else base[other] * sq
            for e in range(2):
                diff = new[e][2 + other] * sq
                if first:
                    diff += base[other] * (off * (k + mid))
                tab[1 + 3 * e, 10 + i] = new[e][other] * sq
                tab[2 + 3 * e, 10 + i] = diff
        if first:
            for c in range(2):
                nrm[c] = root(corner[c] + base[other] * (mid * mid))

        @pl.loop(0, 5)
        def _(j):
            point = lambda i: (i * 5 + j) if along == 0 else (j * 5 + i)
            shared = tab[0, 10 + j]
            norms = []
            if not first:
                for c in range(2):
                    norms.append([root(tab[0, c * 5 + i] + shared) for i in range(5)])
            for e in range(2):
                norm_o, diff_o = tab[1 + 3 * e, 10 + j], tab[2 + 3 * e, 10 + j]
                real, imag = [], []
                for c in range(2):
                    rr, ii = [], []
                    for i in range(5):
                        at = c * 5 + i
                        old = nrm[c] if first else norms[c][i]
                        theta = tab[3 + 3 * e, at] + (tab[2 + 3 * e, at] + diff_o) * inverse(
                            root(tab[1 + 3 * e, at] + norm_o) + old
                        )
                        if first:
                            theta = theta + shared
                        cs, sn = turn(theta)
                        vr, vi = load(c, 0, point(i)), load(c, 1, point(i))
                        rr.append(vr * cs - vi * sn)
                        ii.append(vr * sn + vi * cs)
                    real.append(rr)
                    imag.append(ii)
                for comp, terms in ((0, real), (1, imag)):
                    out = interpolate(terms[0], terms[1])
                    for i in range(5):
                        dst[comp * NODES + point(i), pl.ds(8 * e, 8), :] = out[i]

    def evaluate(p, src):
        k1 = [center((2 * p + q_bit) * 8 + gi, 512.0) + 512.0 * z for z in Z]
        k2 = [center(box2 * 4 + gj, 512.0) + 512.0 * z for z in Z]
        x1 = xa1 + (m0 - 0.5) * h1 + (m2 - 0.5) * h2
        x2 = [xa2 + (m1 - 0.5) * h1 + (h - 0.5) * h2 for h in range(2)]
        speed = [speeds(x1, x2[h]) for h in range(2)]
        for i in range(5):
            tab[0, i] = k1[i]
            tab[0, 5 + i] = k2[i]
            tab[1, i] = k1[i] * k1[i]
            tab[1, 5 + i] = k2[i] * k2[i]
        for h in range(2):
            t1 = [speed[h][0] * speed[h][0] * (k * k) for k in k1]
            t2 = [speed[h][1] * speed[h][1] * (k * k) for k in k2]
            for i in range(5):
                for j in range(5):
                    nrm[h * NODES + i * 5 + j] = root(t1[i] + t2[j])

        for f in range(EV):
            d1, d2 = h2 * POINTS[f][0], h2 * POINTS[f][1]
            new = [moved(x1, x2[h], speed[h][0], speed[h][1], d1, d2) for h in range(2)]
            line1 = [tab[0, i] * d1 for i in range(5)]
            line2 = [tab[0, 5 + i] * d2 for i in range(5)]
            for h in range(2):
                a = new[h]
                n1 = [a[0] * tab[1, i] for i in range(5)]
                n2 = [a[1] * tab[1, 5 + i] for i in range(5)]
                g1 = [a[2] * tab[1, i] for i in range(5)]
                g2 = [a[3] * tab[1, 5 + i] for i in range(5)]
                real, imag = None, None
                for i in range(5):
                    for j in range(5):
                        t = i * 5 + j
                        theta = (line1[i] + line2[j]) + (g1[i] + g2[j]) * inverse(
                            root(n1[i] + n2[j]) + nrm[h * NODES + t]
                        )
                        cs, sn = turn(theta)
                        vr, vi = src[t, pl.ds(8 * h, 8), :], src[NODES + t, pl.ds(8 * h, 8), :]
                        rr = vr * cs - vi * sn
                        ii = vr * sn + vi * cs
                        real = rr if real is None else real + rr
                        imag = ii if imag is None else imag + ii
                acc[2 * f, pl.ds(8 * h, 8), :] += real
                acc[2 * f + 1, pl.ds(8 * h, 8), :] += imag

    acc[...] = jnp.zeros_like(acc)

    def work(p):
        def arrived(c, comp, t):
            return recv[pl.ds(c * SLOT + p * ROWS + comp * NODES + t, 8, stride=2 * SLOT), :]

        def held(src):
            return lambda c, comp, t: src[comp * NODES + t, pl.ds(c, 8, stride=2), :]

        split(0, p, arrived, st0)
        split(1, p, held(st0), st1)
        split(2, p, held(st1), st0)
        split(3, p, held(st0), st1)
        evaluate(p, st1)

    @pl.loop(0, 2)
    def _(p):
        @pl.when(p == 0)
        def _():
            own(0).wait()
            for k in order:
                exchange(0, k).wait()

        @pl.when(p == 1)
        def _():
            own(1).wait()
            for k in order:
                exchange(1, k).wait()

        work(p)

    for h in range(2):
        level = [acc[g, pl.ds(8 * h, 8), :] for g in range(16)]
        for l_bit, by_lane in ((l6, 64), (l5, 32), (l4, 16), (l3, 8)):
            count = len(level) // 2
            merged = []
            for g in range(count):
                u, v = level[g], level[g + count]
                keep = jnp.where(l_bit == 0, u, v)
                give = jnp.where(l_bit == 0, v, u)
                merged.append(
                    keep + jnp.where(l_bit == 0, pltpu.roll(give, 128 - by_lane, 1), pltpu.roll(give, by_lane, 1))
                )
            level = merged
        total = level[0] * (1.0 / (P_SIZE * LEVEL_BOXES))
        for e in range(8):
            part[8 * h + e] = total[e : e + 1, :]

    def hand(e, half):
        e4, e3, e2, e1 = (e >> 3) & 1, (e >> 2) & 1, (e >> 1) & 1, e & 1
        return pltpu.make_async_remote_copy(
            src_ref=part.at[e],
            dst_ref=final.at[slot],
            send_sem=fs_sem.at[e, half],
            recv_sem=fr_sem.at[slot],
            device_id=(4 * line1 + 2 * e3 + e1, 4 * (2 * b0 + half) + 2 * e4 + e2),
            device_id_type=MESH,
        )

    def mine(e, half):
        return is_self & (me == e) & (my_half == half)

    for e in range(16):
        for half in range(2):

            @pl.when(jnp.logical_not(mine(e, half)))
            def _():
                hand(e, half).start()

    @pl.when(is_self)
    def _():
        final[slot] = part[me]

    @pl.loop(0, 32)
    def _(g):
        @pl.when(jnp.logical_not(is_self & (g == slot)))
        def _():
            pltpu.make_async_remote_copy(
                src_ref=part.at[0],
                dst_ref=final.at[g],
                send_sem=fs_sem.at[0, 0],
                recv_sem=fr_sem.at[g],
                device_id=((g // 4) * 4 + source_x, (g % 4) * 4 + source_y),
                device_id_type=MESH,
            ).wait_recv()

    total = final[0]
    for g in range(1, 32):
        total = total + final[g]
    total = jnp.where(my_half == 1, pltpu.roll(total, 124, 1), total)
    for g in range(16):
        row = total if g == 0 else pltpu.roll(total, 128 - 8 * g, 1)
        o_ref[g // 2, g % 2] = row[:, :4]

    for e in range(16):
        for half in range(2):

            @pl.when(jnp.logical_not(mine(e, half)))
            def _():
                hand(e, half).wait_send()


def local(weights):
    vmem = pltpu.VMEM
    dma = pltpu.SemaphoreType.DMA
    return pl.pallas_call(
        kernel,
        out_shape=jax.ShapeDtypeStruct((EV, 2, 1, 4), jnp.float32),
        in_specs=[pl.BlockSpec(memory_space=vmem)],
        out_specs=pl.BlockSpec(memory_space=vmem),
        scratch_shapes=[
            vmem((16 * SLOT, 128), jnp.float32),
            vmem((16 * SLOT, 128), jnp.float32),
            vmem((ROWS, 16, 128), jnp.float32),
            vmem((ROWS, 16, 128), jnp.float32),
            vmem((7, 15, 8, 128), jnp.float32),
            vmem((ROWS, 8, 128), jnp.float32),
            vmem((16, 16, 128), jnp.float32),
            vmem((16, 1, 128), jnp.float32),
            vmem((32, 1, 128), jnp.float32),
            dma((2, 16)),
            dma((2, 16)),
            dma((2,)),
            dma((16, 2)),
            dma((32,)),
        ],
        compiler_params=pltpu.CompilerParams(
            collective_id=0, has_side_effects=True, vmem_limit_bytes=48 * 1024 * 1024
        ),
    )(weights.reshape(ROWS, 4, 8, 128))


def solution(mesh):
    return jax.shard_map(
        local,
        mesh=mesh,
        in_specs=(P(None, None, "bx", "by", None),),
        out_specs=P(None, None, "bx", "by"),
        check_vma=False,
    )
```

profile of v0, /device:TPU:1, one launch (start us, length us, event | category | flops | bytes accessed | tf_op | source)
XLA Modules:
  0.0 57.2 jit_solution(15599330947602312105)
XLA Ops:
  0.0 0.0 copy-start
  0.0 1.1 %copy-done = f32[2,25,4,8,128]{4,3,2,1,0:T(8,128)S(1)} copy-done((f32[2,25,4,8,128]{4,3,2,1,0:T(8,128)S(1)}, f32[2,25,4,8,128]{4,3,2,1,0:T(8,128)}, u32[]{:S(2)}) %copy-start) | copy-done | bytes 819224
  1.1 55.4 %shard_map.17 = f32[8,2,1,4]{3,2,1,0:T(1,128)S(1)} custom-call(f32[50,4,8,128]{3,2,1,0:T(8,128)S(1)} %bitcast.1), custom_call_target="tpu_custom_call" | custom-call | tf_op jit(solution)/shard_map/pallas_call | solution.py:455
  56.5 0.7 %copy.2 = f32[8,2,1,4]{0,3,2,1:T(4,128)} copy(f32[8,2,1,4]{3,2,1,0:T(1,128)S(1)} %shard_map.17) | data formatting | bytes 512 | tf_op jit(solution)/shard_map/pallas_call | solution.py:455
Async XLA Ops:
  0.0 1.1 %copy-start = (f32[2,25,4,8,128]{4,3,2,1,0:T(8,128)S(1)}, f32[2,25,4,8,128]{4,3,2,1,0:T(8,128)}, u32[]{:S(2)}) copy-start(f32[2,25,4,8,128]{4,3,2,1,0:T(8,128)} %param.1) | copy-start | bytes 2457604
where the time goes:
time: 57.4 us; the launch traced here: 57.2 us
  Pallas kernels  55.4 us (97%)
  local copies, waits for them, and re-layouts  1.82 us (3%)
    pallas_call x1, Pallas kernels, local(): pl.pallas_call(kernel, out_shape=jax.ShapeDtypeStruct((EV, 2, 1, 4), jnp....  55.4 us

commit v1 on v0

v1 whole, which is shorter than its diff:
```python
import functools
import math

import jax
import jax.numpy as jnp
import numpy as np
from jax import lax
from jax.experimental import pallas as pl
from jax.experimental.pallas import tpu as pltpu
from jax.sharding import PartitionSpec as P

N = 16384
P_SIZE = 5
LEVEL_BOXES = 128
EV = 8
NODES = P_SIZE * P_SIZE
ROWS = 2 * NODES
PHASES = 4
SLOT = 104
PIECES = ((0, 32), (32, 24), (56, 24), (80, 24))
FAR = ((4, 0), (8, 0), (16, 0), (0, 4), (0, 8))
MESH = pl.DeviceIdType.MESH

SIN = (4.44288292, -7.3082457, 3.60635441, -0.84611289, 0.10982699)
COS = (1.4142135, -6.97885099, 5.73946117, -1.88356299, 0.31069819)


def nodes():
    return np.cos(np.pi * (2.0 * np.arange(P_SIZE) + 1.0) / (2.0 * P_SIZE)) / 2.0


def lower_table():
    z = nodes()
    child = -0.25 + z / 2.0
    table = np.ones((P_SIZE, P_SIZE))
    for m in range(P_SIZE):
        for j in range(P_SIZE):
            if j != m:
                table[m] *= (child - z[j]) / (z[m] - z[j])
    return table


Z = [float(v) for v in nodes()]
LOW = lower_table()
POINTS = [((f + 0.5) / EV - 0.5, ((3 * f) % EV + 0.5) / EV - 0.5) for f in range(EV)]


def turn(theta):
    u = theta - jnp.round(theta)
    w = u * u
    s = SIN[4]
    c = COS[4]
    for k in (3, 2, 1, 0):
        s = s * w + SIN[k]
        c = c * w + COS[k]
    s = s * u
    return 1.0 - s * s, s * c


def interpolate(low, high):
    even = [low[j] + high[4 - j] for j in range(5)]
    odd = [low[j] - high[4 - j] for j in range(5)]
    out = [None] * 5
    for m in (0, 1):
        a = sum_of(even, [0.5 * (LOW[m, j] + LOW[4 - m, j]) for j in range(5)])
        b = sum_of(odd, [0.5 * (LOW[m, j] - LOW[4 - m, j]) for j in range(5)])
        out[m] = a + b
        out[4 - m] = a - b
    out[2] = sum_of(even, [LOW[2, j] for j in range(5)])
    return out


def sum_of(values, factors):
    total = None
    for v, f in zip(values, factors):
        if abs(f) < 1e-14:
            continue
        term = v * float(f)
        total = term if total is None else total + term
    return total


def speeds(x1, x2):
    cp, _ = turn(x1 - x2)
    cq, _ = turn(x1 + x2)
    return (2.0 + 0.5 * (cp - cq)) * 0.0625, (2.0 + 0.5 * (cp + cq)) * 0.0625


def moved(x1, x2, c1, c2, d1, d2, sign=None):
    dp, dq = d1 - d2, d1 + d2
    half = 0.5 if sign is None else 0.5 * sign
    _, sp = turn(x1 - x2 + half * dp)
    _, sq = turn(x1 + x2 + half * dq)
    gp = sp * (-2.0 * math.sin(math.pi * dp))
    gq = sq * (-2.0 * math.sin(math.pi * dq))
    e1 = (gp - gq) * 0.03125
    e2 = (gp + gq) * 0.03125
    if sign is not None:
        e1, e2 = e1 * sign, e2 * sign
    n1, n2 = c1 + e1, c2 + e2
    return n1 * n1, n2 * n2, e1 * (c1 + n1), e2 * (c2 + n2)


def root(s):
    return s * lax.rsqrt(s)


def inverse(s):
    return pltpu.reciprocal(s, approx=True)


def kernel(w_hbm, o_ref, w_ref, send, recv, st0, st1, geo, acc, part, final,
           load_sem, send_sem, recv_sem, own_sem, far_sem, fs_sem, fr_sem):
    bx, by = lax.axis_index("bx"), lax.axis_index("by")
    gi, gj = bx // 4, by // 4
    b0, b1 = bx % 2, (bx // 2) % 2
    c0, c1 = by % 2, (by // 2) % 2
    me = b0 + 2 * c0 + 4 * b1 + 8 * c1
    mine_d = (16 - me) % 16
    slot = gi * 4 + gj
    source = (16 - (2 * gi + gj // 2)) % 16
    source_x, source_y = source % 2 + 2 * ((source // 4) % 2), (source // 2) % 2 + 2 * (source // 8)
    my_half = gj % 2
    is_self = source == me

    load = pltpu.make_async_copy(w_hbm, w_ref, load_sem)
    load.start()

    def peer(k):
        flip = lambda bit, at: (1 - bit) if (k >> at) & 1 else bit
        q0, r0, q1, r1 = flip(b0, 0), flip(c0, 1), flip(b1, 2), flip(c1, 3)
        return q0 + 2 * r0 + 4 * q1 + 8 * r1, (gi * 4 + q0 + 2 * q1, gj * 4 + r0 + 2 * r1)

    def far(n):
        def flip(v, size):
            return v + size * (1 - 2 * ((v // size) % 2)) if size else v

        return flip(bx, FAR[n][0]), flip(by, FAR[n][1])

    order = [k for k in range(16) if k & 2] + [k for k in range(1, 16) if not k & 2]

    barrier = pltpu.get_barrier_semaphore()
    for k in order:
        pl.semaphore_signal(barrier, inc=1, device_id=peer(k)[1], device_id_type=MESH)
    for n in range(5):
        pl.semaphore_signal(barrier, inc=1, device_id=far(n), device_id_type=MESH)

    def far_signal(n):
        pl.semaphore_signal(far_sem.at[n], inc=1, device_id=far(n), device_id_type=MESH)

    def far_wait(n):
        pl.semaphore_wait(far_sem.at[n], 1)

    lane = lax.broadcasted_iota(jnp.int32, (8, 128), 1)
    sub = lax.broadcasted_iota(jnp.int32, (8, 128), 0)
    bit = lambda v, at: (v >> at) & 1
    s2, s1, s0 = (bit(sub, at) for at in (2, 1, 0))
    l6, l5, l4, l3 = (bit(lane, at) for at in (6, 5, 4, 3))

    def shuffle(r):
        phase, t = r // NODES, r % NODES
        a = pltpu.roll(w_ref[t, phase], 0, 1, stride=8, stride_axis=0)
        b = pltpu.roll(w_ref[NODES + t, phase], 64, 1, stride=8, stride_axis=0)
        for by_row, l_bit in ((1, l3), (2, l4), (4, l5)):
            ra, rb = pltpu.roll(a, 8 - by_row, 0), pltpu.roll(b, 8 - by_row, 0)
            wraps = sub >= 8 - by_row
            go, wrap = (l_bit == 1) & jnp.logical_not(wraps), (l_bit == 1) & wraps
            a, b = jnp.where(go, ra, jnp.where(wrap, rb, a)), jnp.where(go, rb, jnp.where(wrap, ra, b))
        a, b = jnp.where(l6 == 1, b, a), jnp.where(l6 == 1, a, b)
        send[pl.ds(r, 8, stride=SLOT), :] = a
        send[pl.ds(8 * SLOT + r, 8, stride=SLOT), :] = b

    def exchange(p, k):
        at, device = peer(k)
        start, count = PIECES[p]
        return pltpu.make_async_remote_copy(
            src_ref=send.at[pl.ds(pl.multiple_of(at * SLOT + start, 8), count)],
            dst_ref=recv.at[pl.ds(pl.multiple_of(me * SLOT + start, 8), count)],
            send_sem=send_sem.at[p, k],
            recv_sem=recv_sem.at[p, k],
            device_id=device,
            device_id_type=MESH,
        )

    def own(p):
        start, count = PIECES[p]
        rows = pl.ds(pl.multiple_of(me * SLOT + start, 8), count)
        return pltpu.make_async_copy(send.at[rows], recv.at[rows], own_sem.at[p])

    load.wait()
    for p in range(PHASES):
        start, count = PIECES[p]

        @pl.loop(start // 4, min(start + count, PHASES * NODES) // 4)
        def _(g):
            for u in range(4):
                shuffle(g * 4 + u)

        if p == 0:
            pl.semaphore_wait(barrier, 20)
        for k in order:
            exchange(p, k).start()
        own(p).start()
        if p == 0:
            far_signal(0)

    f32 = lambda v: v.astype(jnp.float32)
    source_row = ((lane >> 3) + (16 - mine_d)) & 15
    box2 = source_row & 7
    last = source_row >> 3
    line1 = mine_d // 2
    line2 = 8 * (mine_d % 2) + (lane & 7)
    xa1 = (f32(jnp.zeros_like(lane) + ((17 * line1 + 3) % 128)) + 0.5) * (1.0 / 128)
    xa2 = (f32((29 * line2 + 11) & 127) + 0.5) * (1.0 / 128)
    m2, m1, m0 = f32(s2) - 0.5, f32(s1) - 0.5, f32(s0) - 0.5
    m3 = f32(last) - 0.5
    h1, h2 = 1.0 / 256, 1.0 / 512
    places = (
        (xa1, xa2),
        (xa1 + m1 * h1, xa2),
        (xa1 + m0 * h1, xa2 + m1 * h1),
        (xa1 + m0 * h1 + m2 * h2, xa2 + m1 * h1),
        (xa1 + m0 * h1 + m2 * h2, xa2 + m1 * h1 + m3 * h2),
    )
    signs = tuple(2.0 * m for m in (m2, m2, m2, m3))
    steps = (0.5 * h1, 0.5 * h1, 0.5 * h2, 0.5 * h2)

    def center(index, width):
        return f32(index) * width + (0.5 * width - N / 2.0)

    def prepare():
        for level in range(4):
            x, d = places[level], steps[level]
            c = speeds(*x)
            shift = (d, 0.0) if level % 2 == 0 else (0.0, d)
            for n, v in enumerate((c[0] * c[0], c[1] * c[1]) + moved(*x, *c, *shift, signs[level])):
                geo[6 * level + n] = v
        x = places[4]
        c = speeds(*x)
        geo[24], geo[25] = c[0] * c[0], c[1] * c[1]
        for f in range(EV):
            for n, v in enumerate(moved(*x, *c, h2 * POINTS[f][0], h2 * POINTS[f][1])):
                geo[26 + 4 * f + n] = v

    def split(level, p, load, store):
        first = level == 0
        along = level % 2
        other = 1 - along
        if level == 0:
            index = [lambda c: p * 32 + 4 * gi + 2 * s1 + c, lambda c: box2 * 16 + 4 * gj + 2 * last + s0]
            widths = (128.0, 128.0)
        elif level == 1:
            index = [lambda c: p * 16 + 2 * gi + s0, lambda c: box2 * 16 + 4 * gj + 2 * last + c]
            widths = (256.0, 128.0)
        elif level == 2:
            index = [lambda c: jnp.zeros_like(lane) + (p * 16 + 2 * gi + c), lambda c: box2 * 8 + 2 * gj + last]
            widths = (256.0, 256.0)
        else:
            index = [lambda c: jnp.zeros_like(lane) + (p * 8 + gi), lambda c: box2 * 8 + 2 * gj + c]
            widths = (512.0, 256.0)
        base = (geo[6 * level], geo[6 * level + 1])
        new = (geo[6 * level + 2], geo[6 * level + 3])
        more = (geo[6 * level + 4], geo[6 * level + 5])
        step = signs[level] * steps[level]
        x = places[level]

        def table(dim, c):
            mid = center(index[dim](c), widths[dim])
            old, norm, diff, line = [], [], [], []
            for i in range(5):
                off = widths[dim] * Z[i]
                k = mid + off
                sq = k * k
                norm.append(new[dim] * sq)
                if first:
                    diff.append(more[dim] * sq + base[dim] * (off * (k + mid)))
                    line.append(step * mid + (x[dim] + step) * off if dim == along else x[dim] * off)
                else:
                    old.append(base[dim] * sq)
                    diff.append(more[dim] * sq)
                    line.append(step * k if dim == along else None)
            if first:
                old = base[dim] * (mid * mid)
            return old, norm, diff, line

        side = table(other, 0)
        main = [table(along, c) for c in range(2)]
        fixed = [root(main[c][0] + side[0]) for c in range(2)] if first else None
        for j in range(5):
            point = lambda i: (i * 5 + j) if along == 0 else (j * 5 + i)
            real, imag = [], []
            for c in range(2):
                rr, ii = [], []
                old, norm, diff, line = main[c]
                for i in range(5):
                    here = fixed[c] if first else root(old[i] + side[0][j])
                    theta = line[i] + (diff[i] + side[2][j]) * inverse(root(norm[i] + side[1][j]) + here)
                    if first:
                        theta = theta + side[3][j]
                    cs, sn = turn(theta)
                    vr, vi = load(c, point(i))
                    rr.append(vr * cs - vi * sn)
                    ii.append(vr * sn + vi * cs)
                real.append(rr)
                imag.append(ii)
            for comp, terms in ((0, real), (1, imag)):
                out = interpolate(terms[0], terms[1])
                for i in range(5):
                    store(comp, point(i), out[i])

    def evaluate(p, src):
        mid1 = center(jnp.zeros_like(lane) + (p * 8 + gi), 512.0)
        mid2 = center(box2 * 4 + gj, 512.0)
        k1 = [mid1 + 512.0 * z for z in Z]
        k2 = [mid2 + 512.0 * z for z in Z]
        sq1 = [k * k for k in k1]
        sq2 = [k * k for k in k2]
        for i in range(5):
            for j in range(5):
                st0[i * 5 + j, pl.ds(0, 8), :] = root(geo[24] * sq1[i] + geo[25] * sq2[j])
        for f in range(EV):
            d1, d2 = h2 * POINTS[f][0], h2 * POINTS[f][1]
            a = [geo[26 + 4 * f + n] for n in range(4)]
            n1, n2 = [a[0] * v for v in sq1], [a[1] * v for v in sq2]
            g1, g2 = [a[2] * v for v in sq1], [a[3] * v for v in sq2]
            line1, line2 = [d1 * k for k in k1], [d2 * k for k in k2]
            real, imag = acc[2 * f], acc[2 * f + 1]
            for i in range(5):
                for j in range(5):
                    t = i * 5 + j
                    theta = (line1[i] + line2[j]) + (g1[i] + g2[j]) * inverse(
                        root(n1[i] + n2[j]) + st0[t, pl.ds(0, 8), :]
                    )
                    cs, sn = turn(theta)
                    vr, vi = src[t, pl.ds(0, 8), :], src[NODES + t, pl.ds(0, 8), :]
                    real = real + (vr * cs - vi * sn)
                    imag = imag + (vr * sn + vi * cs)
            acc[2 * f], acc[2 * f + 1] = real, imag

    def work(p):
        lower = sub < 4

        def arrived(c, t):
            v = recv[pl.ds(c * SLOT + p * NODES + t, 8, stride=2 * SLOT), :]
            turned = pltpu.roll(v, 4, 0)
            u0, u1 = jnp.where(lower, v, turned), jnp.where(lower, turned, v)
            return jnp.where(last == 0, u0, pltpu.roll(u1, 64, 1)), jnp.where(last == 0, pltpu.roll(u0, 64, 1), u1)

        def held(src):
            return lambda c, t: tuple(src[q * NODES + t, pl.ds(c, 8, stride=2), :] for q in range(2))

        def across(src):
            def load(c, t):
                v = [src[q * NODES + t, pl.ds(0, 8), :] for q in range(2)]
                return tuple(jnp.where(last == c, u, pltpu.roll(u, 64, 1)) for u in v)

            return load

        def twice(dst):
            def store(q, t, v):
                dst[q * NODES + t, pl.ds(0, 8), :] = v
                dst[q * NODES + t, pl.ds(8, 8), :] = v

            return store

        def once(dst):
            def store(q, t, v):
                dst[q * NODES + t, pl.ds(0, 8), :] = v

            return store

        split(0, p, arrived, twice(st0))
        split(1, p, held(st0), twice(st1))
        split(2, p, held(st1), once(st0))
        split(3, p, across(st0), once(st1))
        evaluate(p, st1)

    acc[...] = jnp.zeros_like(acc)
    prepare()

    @pl.loop(0, PHASES)
    def _(p):
        for q in range(PHASES):

            @pl.when(p == q)
            def _():
                own(q).wait()
                for k in order:
                    exchange(q, k).wait_recv()
                far_wait(q)
                far_signal(q + 1)

        work(p)

    level = [pltpu.roll(acc[g], (16 - mine_d) * 8, 1) for g in range(16)]
    for l_bit, by_lane in ((l5, 32), (l4, 16), (l3, 8)):
        count = len(level) // 2
        merged = []
        for g in range(count):
            u, v = level[g], level[g + count]
            keep = jnp.where(l_bit == 0, u, v)
            give = jnp.where(l_bit == 0, v, u)
            merged.append(
                keep + jnp.where(l_bit == 0, pltpu.roll(give, 128 - by_lane, 1), pltpu.roll(give, by_lane, 1))
            )
        level = merged
    level = [v * (1.0 / (P_SIZE * LEVEL_BOXES)) for v in level]
    totals = (
        jnp.where(l6 == 0, level[0], pltpu.roll(level[1], 64, 1)),
        jnp.where(l6 == 0, pltpu.roll(level[0], 64, 1), level[1]),
    )
    for h in range(2):
        for e in range(8):
            part[8 * h + e] = totals[h][e : e + 1, :]

    def hand(e, half):
        e4, e3, e2, e1 = (e >> 3) & 1, (e >> 2) & 1, (e >> 1) & 1, e & 1
        return pltpu.make_async_remote_copy(
            src_ref=part.at[e],
            dst_ref=final.at[slot],
            send_sem=fs_sem.at[e, half],
            recv_sem=fr_sem.at[slot],
            device_id=(4 * line1 + 2 * e3 + e1, 4 * (2 * (mine_d % 2) + half) + 2 * e4 + e2),
            device_id_type=MESH,
        )

    def mine(e, half):
        return is_self & (me == e) & (my_half == half)

    far_wait(4)
    for e in range(16):
        for half in range(2):

            @pl.when(jnp.logical_not(mine(e, half)))
            def _():
                hand(e, half).start()

    @pl.when(is_self)
    def _():
        final[slot] = part[me]

    for p in range(PHASES):
        for k in order:
            exchange(p, k).wait_send()

    @pl.loop(0, 32)
    def _(g):
        @pl.when(jnp.logical_not(is_self & (g == slot)))
        def _():
            pltpu.make_async_remote_copy(
                src_ref=part.at[0],
                dst_ref=final.at[g],
                send_sem=fs_sem.at[0, 0],
                recv_sem=fr_sem.at[g],
                device_id=((g // 4) * 4 + source_x, (g % 4) * 4 + source_y),
                device_id_type=MESH,
            ).wait_recv()

    total = final[0]
    for g in range(1, 32):
        total = total + final[g]
    total = jnp.where(my_half == 1, pltpu.roll(total, 124, 1), total)
    for q in range(2):
        for f in range(EV):
            at = 64 * q + 8 * f
            row = total if at == 0 else pltpu.roll(total, 128 - at, 1)
            o_ref[f, q] = row[:, :4]

    for e in range(16):
        for half in range(2):

            @pl.when(jnp.logical_not(mine(e, half)))
            def _():
                hand(e, half).wait_send()


def local(weights):
    vmem = pltpu.VMEM
    dma = pltpu.SemaphoreType.DMA
    return pl.pallas_call(
        kernel,
        out_shape=jax.ShapeDtypeStruct((EV, 2, 1, 4), jnp.float32),
        in_specs=[pl.BlockSpec(memory_space=pl.ANY)],
        out_specs=pl.BlockSpec(memory_space=vmem),
        scratch_shapes=[
            vmem((ROWS, 4, 8, 128), jnp.float32),
            vmem((16 * SLOT, 128), jnp.float32),
            vmem((16 * SLOT, 128), jnp.float32),
            vmem((ROWS, 16, 128), jnp.float32),
            vmem((ROWS, 16, 128), jnp.float32),
            vmem((58, 8, 128), jnp.float32),
            vmem((16, 8, 128), jnp.float32),
            vmem((16, 1, 128), jnp.float32),
            vmem((32, 1, 128), jnp.float32),
            dma(()),
            dma((PHASES, 16)),
            dma((PHASES, 16)),
            dma((PHASES,)),
            pltpu.SemaphoreType.REGULAR((5,)),
            dma((16, 2)),
            dma((32,)),
        ],
        compiler_params=pltpu.CompilerParams(
            collective_id=0, has_side_effects=True, vmem_limit_bytes=60 * 1024 * 1024
        ),
    )(weights.reshape(ROWS, 4, 8, 128))


def solution(mesh):
    return jax.shard_map(
        local,
        mesh=mesh,
        in_specs=(P(None, None, "bx", "by", None),),
        out_specs=P(None, None, "bx", "by"),
        check_vma=False,
    )
```

time: 57.4 us -> 52.3 us (0.911)
  Pallas kernels: 55.4 us -> 50.7 us
    pallas_call x1, Pallas kernels: 55.4 us -> 50.7 us  [local(): pl.pallas_call(kernel, out_shape=jax.ShapeDtypeStruct((EV, 2, 1, 4), jnp....]
    unnamed x2 -> x0, local copies, waits for them, and re-layouts: 1.14 us -> none
    pallas_call x1, local copies, waits for them, and re-layouts: 0.68 us -> 1.37 us  [local(): pl.pallas_call(kernel, out_shape=jax.ShapeDtypeStruct((EV, 2, 1, 4), jnp....]
where the time goes in v1:
time: 52.3 us; the launch traced here: 52.1 us
  Pallas kernels  50.7 us (97%)
  local copies, waits for them, and re-layouts  1.37 us (3%)
    pallas_call x1, Pallas kernels, local(): pl.pallas_call(kernel, out_shape=jax.ShapeDtypeStruct((EV, 2, 1, 4), jnp....  50.7 us
    pallas_call x1, local copies, waits for them, and re-layouts, local(): pl.pallas_call(kernel, out_shape=jax.ShapeDtypeStruct((EV, 2, 1, 4), jnp....  1.37 us

profile of v1, /device:TPU:1, one launch (start us, length us, event | category | flops | bytes accessed | tf_op | source)
XLA Modules:
  0.0 52.1 jit_solution(9962954209928541132)
XLA Ops:
  0.0 50.7 %shard_map.17 = f32[8,2,1,4]{3,2,1,0:T(1,128)} custom-call(f32[50,4,8,128]{3,2,1,0:T(8,128)} %bitcast.1), custom_call_target="tpu_custom_call" | custom-call | tf_op jit(solution)/shard_map/pallas_call | solution.py:480
  50.7 1.4 %copy.2 = f32[8,2,1,4]{0,3,2,1:T(4,128)} copy(f32[8,2,1,4]{3,2,1,0:T(1,128)} %shard_map.17) | data formatting | bytes 512 | tf_op jit(solution)/shard_map/pallas_call | solution.py:480

commit v2 on v1

v2 whole, which is shorter than its diff:
```python
import functools
import math

import jax
import jax.numpy as jnp
import numpy as np
from jax import lax
from jax.experimental import pallas as pl
from jax.experimental.pallas import tpu as pltpu
from jax.sharding import PartitionSpec as P

N = 16384
P_SIZE = 5
LEVEL_BOXES = 128
EV = 8
NODES = P_SIZE * P_SIZE
ROWS = 2 * NODES
PHASES = 4
WIDE = 2
GAP = 6
SLOT = 112
PIECES = ((0, 32), (32, 24), (56, 32), (88, 24))
PARTS = ((0, 32), (32, 50), (50, 82), (82, 100))
MESH = pl.DeviceIdType.MESH

SIN = (4.44288292, -7.3082457, 3.60635441, -0.84611289, 0.10982699)
COS = (1.4142135, -6.97885099, 5.73946117, -1.88356299, 0.31069819)


def nodes():
    return np.cos(np.pi * (2.0 * np.arange(P_SIZE) + 1.0) / (2.0 * P_SIZE)) / 2.0


def lower_table():
    z = nodes()
    child = -0.25 + z / 2.0
    table = np.ones((P_SIZE, P_SIZE))
    for m in range(P_SIZE):
        for j in range(P_SIZE):
            if j != m:
                table[m] *= (child - z[j]) / (z[m] - z[j])
    return table


Z = [float(v) for v in nodes()]
LOW = lower_table()
POINTS = [((f + 0.5) / EV - 0.5, ((3 * f) % EV + 0.5) / EV - 0.5) for f in range(EV)]


def turn(theta):
    u = theta - jnp.round(theta)
    w = u * u
    s = SIN[4]
    c = COS[4]
    for k in (3, 2, 1, 0):
        s = s * w + SIN[k]
        c = c * w + COS[k]
    s = s * u
    return 1.0 - s * s, s * c


def interpolate_one(values, upper):
    values = [jnp.where(upper == 0, values[j], values[4 - j]) for j in range(5)]
    sign = (1 - 2 * upper).astype(jnp.float32)
    out = [None] * 5
    for m in (0, 1):
        a = sum_of(values, [0.5 * (LOW[m, j] + LOW[4 - m, j]) for j in range(5)])
        b = sum_of(values, [0.5 * (LOW[m, j] - LOW[4 - m, j]) for j in range(5)]) * sign
        out[m] = a + b
        out[4 - m] = a - b
    out[2] = sum_of(values, [LOW[2, j] for j in range(5)])
    return out


def interpolate(low, high):
    even = [low[j] + high[4 - j] for j in range(5)]
    odd = [low[j] - high[4 - j] for j in range(5)]
    out = [None] * 5
    for m in (0, 1):
        a = sum_of(even, [0.5 * (LOW[m, j] + LOW[4 - m, j]) for j in range(5)])
        b = sum_of(odd, [0.5 * (LOW[m, j] - LOW[4 - m, j]) for j in range(5)])
        out[m] = a + b
        out[4 - m] = a - b
    out[2] = sum_of(even, [LOW[2, j] for j in range(5)])
    return out


def sum_of(values, factors):
    total = None
    for v, f in zip(values, factors):
        if abs(f) < 1e-14:
            continue
        term = v * float(f)
        total = term if total is None else total + term
    return total


def speeds(x1, x2):
    cp, _ = turn(x1 - x2)
    cq, _ = turn(x1 + x2)
    return (2.0 + 0.5 * (cp - cq)) * 0.0625, (2.0 + 0.5 * (cp + cq)) * 0.0625


def moved(x1, x2, c1, c2, d1, d2, sign=None):
    dp, dq = d1 - d2, d1 + d2
    half = 0.5 if sign is None else 0.5 * sign
    _, sp = turn(x1 - x2 + half * dp)
    _, sq = turn(x1 + x2 + half * dq)
    gp = sp * (-2.0 * math.sin(math.pi * dp))
    gq = sq * (-2.0 * math.sin(math.pi * dq))
    e1 = (gp - gq) * 0.03125
    e2 = (gp + gq) * 0.03125
    if sign is not None:
        e1, e2 = e1 * sign, e2 * sign
    n1, n2 = c1 + e1, c2 + e2
    return n1 * n1, n2 * n2, e1 * (c1 + n1), e2 * (c2 + n2)


def root(s):
    return s * lax.rsqrt(s)


def inverse(s):
    return pltpu.reciprocal(s, approx=True)


def kernel(w_hbm, o_ref, w_ref, send, recv, st0, st1, st2, st3, norms, geo, lanes, acc, gift_out, gift_in, part, final,
           load_sem, send_sem, recv_sem, own_sem, far_sem, gift_sem, fs_sem, fr_sem):
    bx, by = lax.axis_index("bx"), lax.axis_index("by")
    gi, gj = bx // 4, by // 4
    b0, b1 = bx % 2, (bx // 2) % 2
    c0, c1 = by % 2, (by // 2) % 2
    me = b0 + 2 * c0 + 4 * b1 + 8 * c1
    mine_d = (16 - me) % 16
    slot = gi * 4 + gj
    source = (16 - (2 * gi + gj // 2)) % 16
    source_x, source_y = source % 2 + 2 * ((source // 4) % 2), (source // 2) % 2 + 2 * (source // 8)
    my_half = gj % 2
    is_self = source == me

    load = pltpu.make_async_copy(w_hbm, w_ref, load_sem)
    load.start()

    def peer(k):
        flip = lambda bit, at: (1 - bit) if (k >> at) & 1 else bit
        q0, r0, q1, r1 = flip(b0, 0), flip(c0, 1), flip(b1, 2), flip(c1, 3)
        return q0 + 2 * r0 + 4 * q1 + 8 * r1, (gi * 4 + q0 + 2 * q1, gj * 4 + r0 + 2 * r1)

    def flipped(at_x, at_y):
        def flip(v, bits):
            for size in (1, 2, 4, 8, 16):
                if bits & size:
                    v = v + size * (1 - 2 * ((v // size) % 2))
            return v

        return flip(bx, at_x), flip(by, at_y)

    near = [k for k in (4, 12, 5, 13, 8, 9, 1)]
    order = [k for k in range(16) if k & 2] + near

    steps_y = ((4, 0), (4, 1))
    steps_far = ((8, 0), (16, 0), (0, 4), (0, 12))
    barrier = pltpu.get_barrier_semaphore()
    for device in [peer(k)[1] for k in near] + [flipped(*at) for at in steps_y + steps_far]:
        pl.semaphore_signal(barrier, inc=1, device_id=device, device_id_type=MESH)

    def tell(n, at):
        pl.semaphore_signal(far_sem.at[n], inc=1, device_id=flipped(*at), device_id_type=MESH)

    def told(n):
        pl.semaphore_wait(far_sem.at[n], 1)

    lane = lax.broadcasted_iota(jnp.int32, (8, 128), 1)
    sub = lax.broadcasted_iota(jnp.int32, (8, 128), 0)
    bit = lambda v, at: (v >> at) & 1
    s2, s1, s0 = (bit(sub, at) for at in (2, 1, 0))
    l6, l5, l4, l3 = (bit(lane, at) for at in (6, 5, 4, 3))

    def shuffle(n):
        phase, t = n // NODES, n % NODES
        r = n + GAP * (n // (WIDE * NODES))
        a = pltpu.roll(w_ref[t, phase], 0, 1, stride=8, stride_axis=0)
        b = pltpu.roll(w_ref[NODES + t, phase], 64, 1, stride=8, stride_axis=0)
        for by_row, l_bit in ((1, l3), (2, l4), (4, l5)):
            ra, rb = pltpu.roll(a, 8 - by_row, 0), pltpu.roll(b, 8 - by_row, 0)
            wraps = sub >= 8 - by_row
            go, wrap = (l_bit == 1) & jnp.logical_not(wraps), (l_bit == 1) & wraps
            a, b = jnp.where(go, ra, jnp.where(wrap, rb, a)), jnp.where(go, rb, jnp.where(wrap, ra, b))
        a, b = jnp.where(l6 == 1, b, a), jnp.where(l6 == 1, a, b)
        send[pl.ds(r, 8, stride=SLOT), :] = a
        send[pl.ds(8 * SLOT + r, 8, stride=SLOT), :] = b

    def exchange(p, k):
        start, count = PIECES[p]
        at, device = peer(k)
        place = me
        if p < WIDE:
            device = peer(k & 13)[1]
            place = b0 + (k & 2) + 4 * b1 + 8 * c1
        return pltpu.make_async_remote_copy(
            src_ref=send.at[pl.ds(pl.multiple_of(at * SLOT + start, 8), count)],
            dst_ref=recv.at[pl.ds(pl.multiple_of(place * SLOT + start, 8), count)],
            send_sem=send_sem.at[p, k],
            recv_sem=recv_sem.at[p, k],
            device_id=device,
            device_id_type=MESH,
        )

    def own(p, k):
        start, count = PIECES[p]
        at = peer(k)[0]
        place = b0 + k + 4 * b1 + 8 * c1 if p < WIDE else me
        return pltpu.make_async_copy(
            send.at[pl.ds(pl.multiple_of(at * SLOT + start, 8), count)],
            recv.at[pl.ds(pl.multiple_of(place * SLOT + start, 8), count)],
            own_sem.at[p, k // 2],
        )

    wide_order = [k | more for k in near for more in (0, 2)]
    orders = [wide_order if p < WIDE else order for p in range(PHASES)]
    owns = [(0, 2) if p < WIDE else (0,) for p in range(PHASES)]

    load.wait()
    for p in range(PHASES):
        low, high = PARTS[p]
        unroll = 4 if (high - low) % 4 == 0 else 2

        @pl.loop(0, (high - low) // unroll)
        def _(g):
            for u in range(unroll):
                shuffle(low + g * unroll + u)

        if p == 0:
            pl.semaphore_wait(barrier, 13)
        if p == WIDE:
            told(2)
        for k in orders[p]:
            exchange(p, k).start()
        for k in owns[p]:
            own(p, k).start()
        if p == 0:
            tell(0, steps_y[0])
            tell(1, steps_y[1])
        if p == 1:
            told(0)
            told(1)
            tell(2, steps_y[1])
        if p == 2:
            tell(3, steps_far[0])

    f32 = lambda v: v.astype(jnp.float32)
    m2, m1, m0 = f32(s2) - 0.5, f32(s1) - 0.5, f32(s0) - 0.5
    h1, h2 = 1.0 / 256, 1.0 / 512
    steps = (0.5 * h1, 0.5 * h1, 0.5 * h2, 0.5 * h2)
    other_d = (16 - peer(2)[0]) % 16

    def lines(d):
        d = jnp.zeros_like(lane) + d
        source_row = ((lane >> 3) + (16 - d)) & 15
        line2 = 8 * (d & 1) + (lane & 7)
        xa1 = (f32((17 * (d >> 1) + 3) & 127) + 0.5) * (1.0 / 128)
        xa2 = (f32((29 * line2 + 11) & 127) + 0.5) * (1.0 / 128)
        return source_row & 7, source_row >> 3, xa1, xa2

    def center(index, width):
        return f32(index) * width + (0.5 * width - N / 2.0)

    def prepare(which, d, levels):
        box2, last, xa1, xa2 = lines(d)
        lanes[which, 0], lanes[which, 1] = box2, last
        m3 = f32(last) - 0.5
        places = (
            (xa1, xa2),
            (xa1 + m1 * h1, xa2),
            (xa1 + m0 * h1, xa2 + m1 * h1),
            (xa1 + m0 * h1 + m2 * h2, xa2 + m1 * h1),
            (xa1 + m0 * h1 + m2 * h2, xa2 + m1 * h1 + m3 * h2),
        )
        for level in levels:
            x, d = places[level], steps[level] if level < 4 else None
            c = speeds(*x)
            if level < 4:
                shift = (d, 0.0) if level % 2 == 0 else (0.0, d)
                sign = 2.0 * (m2 if level < 3 else m3)
                for n, v in enumerate((c[0] * c[0], c[1] * c[1]) + moved(*x, *c, *shift, sign)):
                    geo[which, 6 * level + n] = v
            else:
                geo[which, 24], geo[which, 25] = c[0] * c[0], c[1] * c[1]
                for f in range(EV):
                    for n, v in enumerate(moved(*x, *c, h2 * POINTS[f][0], h2 * POINTS[f][1])):
                        geo[which, 26 + 4 * f + n] = v

    def split(level, p, which, load, store, wide=False):
        box2, last = lanes[which, 0], lanes[which, 1]
        single = wide and level == 1
        below = c0 if wide else s0
        first = level == 0
        along = level % 2
        other = 1 - along
        if level == 0:
            index = [lambda c: p * 32 + 4 * gi + 2 * s1 + c, lambda c: box2 * 16 + 4 * gj + 2 * last + below]
            widths = (128.0, 128.0)
        elif level == 1:
            index = [lambda c: p * 16 + 2 * gi + s0, lambda c: box2 * 16 + 4 * gj + 2 * last + c]
            widths = (256.0, 128.0)
        elif level == 2:
            index = [lambda c: jnp.zeros_like(lane) + (p * 16 + 2 * gi + c), lambda c: box2 * 8 + 2 * gj + last]
            widths = (256.0, 256.0)
        else:
            index = [lambda c: jnp.zeros_like(lane) + (p * 8 + gi), lambda c: box2 * 8 + 2 * gj + c]
            widths = (512.0, 256.0)
        base, new, more = ((geo[which, 6 * level + n], geo[which, 6 * level + n + 1]) for n in (0, 2, 4))
        step = (2.0 * steps[level]) * (m2 if level < 3 else f32(last) - 0.5)
        x = lines(group(which))[2:] if first else None

        def table(dim, c):
            mid = center(index[dim](c), widths[dim])
            old, norm, diff, line = [], [], [], []
            for i in range(5):
                off = widths[dim] * Z[i]
                k = mid + off
                sq = k * k
                norm.append(new[dim] * sq)
                if first:
                    diff.append(more[dim] * sq + base[dim] * (off * (k + mid)))
                    line.append(step * mid + (x[dim] + step) * off if dim == along else x[dim] * off)
                else:
                    old.append(base[dim] * sq)
                    diff.append(more[dim] * sq)
                    line.append(step * k if dim == along else None)
            if first:
                old = base[dim] * (mid * mid)
            return old, norm, diff, line

        side = table(other, 0)
        children = (c0,) if single else (0, 1)
        main = [table(along, c) for c in children]
        fixed = [root(old + side[0]) for old, _, _, _ in main] if first else None
        for j in range(5):
            point = lambda i: (i * 5 + j) if along == 0 else (j * 5 + i)
            real, imag = [], []
            for c in range(len(children)):
                rr, ii = [], []
                old, norm, diff, line = main[c]
                for i in range(5):
                    here = fixed[c] if first else root(old[i] + side[0][j])
                    theta = line[i] + (diff[i] + side[2][j]) * inverse(root(norm[i] + side[1][j]) + here)
                    if first:
                        theta = theta + side[3][j]
                    cs, sn = turn(theta)
                    vr, vi = load(c, point(i))
                    rr.append(vr * cs - vi * sn)
                    ii.append(vr * sn + vi * cs)
                real.append(rr)
                imag.append(ii)
            for comp, terms in ((0, real), (1, imag)):
                out = interpolate_one(terms[0], c0) if single else interpolate(terms[0], terms[1])
                for i in range(5):
                    store(comp, point(i), out[i])

    def evaluate(p, which, src):
        box2 = lanes[which, 0]
        mid1 = center(jnp.zeros_like(lane) + (p * 8 + gi), 512.0)
        mid2 = center(box2 * 4 + gj, 512.0)
        k1 = [mid1 + 512.0 * z for z in Z]
        k2 = [mid2 + 512.0 * z for z in Z]
        sq1 = [k * k for k in k1]
        sq2 = [k * k for k in k2]
        for i in range(5):
            for j in range(5):
                norms[i * 5 + j] = root(geo[which, 24] * sq1[i] + geo[which, 25] * sq2[j])
        for f in range(EV):
            d1, d2 = h2 * POINTS[f][0], h2 * POINTS[f][1]
            a = [geo[which, 26 + 4 * f + n] for n in range(4)]
            n1, n2 = [a[0] * v for v in sq1], [a[1] * v for v in sq2]
            g1, g2 = [a[2] * v for v in sq1], [a[3] * v for v in sq2]
            line1, line2 = [d1 * k for k in k1], [d2 * k for k in k2]
            real, imag = acc[which, 2 * f], acc[which, 2 * f + 1]
            for i in range(5):
                for j in range(5):
                    t = i * 5 + j
                    theta = (line1[i] + line2[j]) + (g1[i] + g2[j]) * inverse(
                        root(n1[i] + n2[j]) + norms[t]
                    )
                    cs, sn = turn(theta)
                    vr, vi = src[t], src[NODES + t]
                    real = real + (vr * cs - vi * sn)
                    imag = imag + (vr * sn + vi * cs)
            acc[which, 2 * f], acc[which, 2 * f + 1] = real, imag

    def group(which):
        if which == 2:
            return jnp.where(s0 == 0, mine_d, other_d)
        return mine_d

    def arrived(p, which, gap):
        last = lanes[which, 1]
        lower = sub < 4

        def load(c, t):
            v = recv[pl.ds(c * SLOT + gap + p * NODES + t, 8, stride=2 * SLOT), :]
            turned = pltpu.roll(v, 4, 0)
            u0, u1 = jnp.where(lower, v, turned), jnp.where(lower, turned, v)
            return jnp.where(last == 0, u0, pltpu.roll(u1, 64, 1)), jnp.where(last == 0, pltpu.roll(u0, 64, 1), u1)

        return load

    def twice(dst):
        def store(q, t, v):
            dst[q * NODES + t, pl.ds(0, 8), :] = v
            dst[q * NODES + t, pl.ds(8, 8), :] = v

        return store

    def once(dst):
        def store(q, t, v):
            dst[q * NODES + t] = v

        return store

    def rest(p, which):
        last = lanes[which, 1]

        def held(c, t):
            return tuple(st1[q * NODES + t, pl.ds(c, 8, stride=2), :] for q in range(2))

        def across(c, t):
            v = [st2[q * NODES + t] for q in range(2)]
            return tuple(jnp.where(last == c, u, pltpu.roll(u, 64, 1)) for u in v)

        split(2, p, which, held, once(st2))
        split(3, p, which, across, once(st3))
        evaluate(p, which, st3)

    def fold(which, d):
        level = [pltpu.roll(acc[which, g], (16 - d) * 8, 1) for g in range(16)]
        for l_bit, by_lane in ((l5, 32), (l4, 16), (l3, 8)):
            count = len(level) // 2
            merged = []
            for g in range(count):
                u, v = level[g], level[g + count]
                keep = jnp.where(l_bit == 0, u, v)
                give = jnp.where(l_bit == 0, v, u)
                merged.append(
                    keep + jnp.where(l_bit == 0, pltpu.roll(give, 128 - by_lane, 1), pltpu.roll(give, by_lane, 1))
                )
            level = merged
        level = [v * (1.0 / (P_SIZE * LEVEL_BOXES)) for v in level]
        return (
            jnp.where(l6 == 0, level[0], pltpu.roll(level[1], 64, 1)),
            jnp.where(l6 == 0, pltpu.roll(level[0], 64, 1), level[1]),
        )

    acc[...] = jnp.zeros_like(acc)
    prepare(2, group(2), (0,))
    prepare(0, mine_d, range(5))
    prepare(1, other_d, range(1, 5))

    def await_piece(q):
        for k in owns[q]:
            own(q, k).wait()
        for k in orders[q]:
            exchange(q, k).wait_recv()

    @pl.loop(0, WIDE)
    def _(p):
        for q in range(WIDE):

            @pl.when(p == q)
            def _():
                await_piece(q)
                told(3 + q)
                tell(4 + q, steps_far[1 + q])

        split(0, p, 2, arrived(p, 2, 0), twice(st0), wide=True)

        @pl.loop(0, 2)
        def _(which):
            def side(c, t):
                return tuple(st0[q * NODES + t, pl.ds(which, 8, stride=2), :] for q in range(2))

            split(1, p, which, side, twice(st1), wide=True)
            rest(p, which)

    gift = pltpu.make_async_remote_copy(
        src_ref=gift_out,
        dst_ref=gift_in,
        send_sem=gift_sem.at[0],
        recv_sem=gift_sem.at[1],
        device_id=flipped(0, 1),
        device_id_type=MESH,
    )
    gift_out[0], gift_out[1] = fold(1, other_d)
    gift.start()

    @pl.loop(WIDE, PHASES)
    def _(p):
        for q in range(WIDE, PHASES):

            @pl.when(p == q)
            def _():
                await_piece(q)
                told(3 + q)
                if q == WIDE:
                    tell(4 + q, steps_far[1 + q])

        def held(c, t):
            return tuple(st0[q * NODES + t, pl.ds(c, 8, stride=2), :] for q in range(2))

        split(0, p, 0, arrived(p, 0, GAP), twice(st0))
        split(1, p, 0, held, twice(st1))
        rest(p, 0)

    gift.wait()
    totals = fold(0, mine_d)
    for h in range(2):
        total = totals[h] + gift_in[h]
        for e in range(8):
            part[8 * h + e] = total[e : e + 1, :]

    line1 = mine_d // 2

    def hand(e, half):
        e4, e3, e2, e1 = (e >> 3) & 1, (e >> 2) & 1, (e >> 1) & 1, e & 1
        return pltpu.make_async_remote_copy(
            src_ref=part.at[e],
            dst_ref=final.at[slot],
            send_sem=fs_sem.at[e, half],
            recv_sem=fr_sem.at[slot],
            device_id=(4 * line1 + 2 * e3 + e1, 4 * (2 * (mine_d % 2) + half) + 2 * e4 + e2),
            device_id_type=MESH,
        )

    def mine(e, half):
        return is_self & (me == e) & (my_half == half)

    for e in range(16):
        for half in range(2):

            @pl.when(jnp.logical_not(mine(e, half)))
            def _():
                hand(e, half).start()

    @pl.when(is_self)
    def _():
        final[slot] = part[me]

    for p in range(PHASES):
        for k in orders[p]:
            exchange(p, k).wait_send()

    @pl.loop(0, 32)
    def _(g):
        @pl.when(jnp.logical_not(is_self & (g == slot)))
        def _():
            pltpu.make_async_remote_copy(
                src_ref=part.at[0],
                dst_ref=final.at[g],
                send_sem=fs_sem.at[0, 0],
                recv_sem=fr_sem.at[g],
                device_id=((g // 4) * 4 + source_x, (g % 4) * 4 + source_y),
                device_id_type=MESH,
            ).wait_recv()

    total = final[0]
    for g in range(1, 32):
        total = total + final[g]
    total = jnp.where(my_half == 1, pltpu.roll(total, 124, 1), total)
    spread = jnp.where((lane & 7) == sub, jnp.broadcast_to(total, (8, 128)), 0.0)
    place = lax.broadcasted_iota(jnp.int32, (128, 128), 0) >> 3
    column = lax.broadcasted_iota(jnp.int32, (128, 128), 1)
    picked = jnp.dot(
        spread,
        jnp.where(place == column, 1.0, 0.0),
        precision=lax.Precision.HIGHEST,
        preferred_element_type=jnp.float32,
    )
    o_ref[0, 0] = picked[:4, :EV]
    o_ref[1, 0] = picked[:4, EV : 2 * EV]

    for e in range(16):
        for half in range(2):

            @pl.when(jnp.logical_not(mine(e, half)))
            def _():
                hand(e, half).wait_send()


def local(weights):
    vmem = pltpu.VMEM
    dma = pltpu.SemaphoreType.DMA
    out = pl.pallas_call(
        kernel,
        out_shape=jax.ShapeDtypeStruct((2, 1, 4, EV), jnp.float32),
        in_specs=[pl.BlockSpec(memory_space=pl.ANY)],
        out_specs=pl.BlockSpec(memory_space=vmem),
        scratch_shapes=[
            vmem((ROWS, 4, 8, 128), jnp.float32),
            vmem((16 * SLOT, 128), jnp.float32),
            vmem((16 * SLOT, 128), jnp.float32),
            vmem((ROWS, 16, 128), jnp.float32),
            vmem((ROWS, 16, 128), jnp.float32),
            vmem((ROWS, 8, 128), jnp.float32),
            vmem((ROWS, 8, 128), jnp.float32),
            vmem((NODES, 8, 128), jnp.float32),
            vmem((3, 58, 8, 128), jnp.float32),
            vmem((3, 2, 8, 128), jnp.int32),
            vmem((2, 16, 8, 128), jnp.float32),
            vmem((2, 8, 128), jnp.float32),
            vmem((2, 8, 128), jnp.float32),
            vmem((16, 1, 128), jnp.float32),
            vmem((32, 1, 128), jnp.float32),
            dma(()),
            dma((PHASES, 16)),
            dma((PHASES, 16)),
            dma((PHASES, 2)),
            pltpu.SemaphoreType.REGULAR((7,)),
            dma((2,)),
            dma((16, 2)),
            dma((32,)),
        ],
        compiler_params=pltpu.CompilerParams(
            collective_id=0, has_side_effects=True, vmem_limit_bytes=60 * 1024 * 1024
        ),
    )(weights.reshape(ROWS, 4, 8, 128))
    return jnp.transpose(out, (3, 0, 1, 2))


def solution(mesh):
    return jax.shard_map(
        local,
        mesh=mesh,
        in_specs=(P(None, None, "bx", "by", None),),
        out_specs=P(None, None, "bx", "by"),
        check_vma=False,
    )
```

time: 52.3 us -> 46.2 us (0.88)
  Pallas kernels: 50.7 us -> 44.8 us
    pallas_call x1, Pallas kernels: 50.7 us -> 44.8 us  [local(): pl.pallas_call(kernel, out_shape=jax.ShapeDtypeStruct((2, 1, 4, EV), jnp....]
    pallas_call x1 -> x0, local copies, waits for them, and re-layouts: 1.37 us -> none  [local(): pl.pallas_call(kernel, out_shape=jax.ShapeDtypeStruct((EV, 2, 1, 4), jnp....]
    unnamed x0 -> x1, local copies, waits for them, and re-layouts: none -> 1.28 us
where the time goes in v2:
time: 46.2 us; the launch traced here: 46.1 us
  Pallas kernels  44.8 us (97%)
  local copies, waits for them, and re-layouts  1.28 us (3%)
    pallas_call x1, Pallas kernels, local(): pl.pallas_call(kernel, out_shape=jax.ShapeDtypeStruct((2, 1, 4, EV), jnp....  44.8 us
    unnamed x1, local copies, waits for them, and re-layouts  1.28 us

profile of v2, /device:TPU:1, one launch (start us, length us, event | category | flops | bytes accessed | tf_op | source)
XLA Modules:
  0.0 46.1 jit_solution(16174483680411026232)
XLA Ops:
  0.0 44.8 %shard_map.17 = f32[2,1,4,8]{3,2,1,0:T(4,128)} custom-call(f32[50,4,8,128]{3,2,1,0:T(8,128)} %bitcast.2), custom_call_target="tpu_custom_call" | custom-call | tf_op jit(solution)/shard_map/pallas_call | solution.py:592
  44.8 1.3 %copy.3 = f32[8,2,1,4]{0,3,2,1:T(4,128)} copy(f32[8,2,1,4]{0,3,2,1:T(4,128)} %bitcast.3) | data formatting | bytes 512

commit v3 on v2

--- a/solution.py
+++ b/solution.py
@@ -17,10 +17,8 @@
 ROWS = 2 * NODES
 PHASES = 4
 WIDE = 2
-GAP = 6
-SLOT = 112
-PIECES = ((0, 32), (32, 24), (56, 32), (88, 24))
-PARTS = ((0, 32), (32, 50), (50, 82), (82, 100))
+STRIDE = 32
+SLOT = PHASES * STRIDE
 MESH = pl.DeviceIdType.MESH
 
 SIN = (4.44288292, -7.3082457, 3.60635441, -0.84611289, 0.10982699)
@@ -178,7 +176,7 @@
 
     def shuffle(n):
         phase, t = n // NODES, n % NODES
-        r = n + GAP * (n // (WIDE * NODES))
+        r = phase * STRIDE + t
         a = pltpu.roll(w_ref[t, phase], 0, 1, stride=8, stride_axis=0)
         b = pltpu.roll(w_ref[NODES + t, phase], 64, 1, stride=8, stride_axis=0)
         for by_row, l_bit in ((1, l3), (2, l4), (4, l5)):
@@ -191,7 +189,7 @@
         send[pl.ds(8 * SLOT + r, 8, stride=SLOT), :] = b
 
     def exchange(p, k):
-        start, count = PIECES[p]
+        start, count = p * STRIDE, NODES
         at, device = peer(k)
         place = me
         if p < WIDE:
@@ -207,7 +205,7 @@
         )
 
     def own(p, k):
-        start, count = PIECES[p]
+        start, count = p * STRIDE, NODES
         at = peer(k)[0]
         place = b0 + k + 4 * b1 + 8 * c1 if p < WIDE else me
         return pltpu.make_async_copy(
@@ -220,33 +218,36 @@
     orders = [wide_order if p < WIDE else order for p in range(PHASES)]
     owns = [(0, 2) if p < WIDE else (0,) for p in range(PHASES)]
 
-    load.wait()
-    for p in range(PHASES):
-        low, high = PARTS[p]
-        unroll = 4 if (high - low) % 4 == 0 else 2
-
-        @pl.loop(0, (high - low) // unroll)
+    def pack(p):
+        @pl.loop(0, 5)
         def _(g):
-            for u in range(unroll):
-                shuffle(low + g * unroll + u)
-
-        if p == 0:
-            pl.semaphore_wait(barrier, 13)
-        if p == WIDE:
-            told(2)
+            for u in range(5):
+                shuffle(p * NODES + g * 5 + u)
+
+    def ship(p):
         for k in orders[p]:
             exchange(p, k).start()
         for k in owns[p]:
             own(p, k).start()
-        if p == 0:
-            tell(0, steps_y[0])
-            tell(1, steps_y[1])
-        if p == 1:
-            told(0)
-            told(1)
-            tell(2, steps_y[1])
-        if p == 2:
-            tell(3, steps_far[0])
+
+    load.wait()
+    pack(0)
+    pl.semaphore_wait(barrier, 13)
+    tell(0, steps_y[0])
+    tell(1, steps_y[1])
+    for p in range(WIDE):
+        if p > 0:
+            pack(p)
+        ship(p)
+    told(0)
+    told(1)
+    tell(2, steps_y[1])
+    for p in range(WIDE, PHASES):
+        pack(p)
+    told(2)
+    for p in range(WIDE, PHASES):
+        ship(p)
+    tell(3, steps_far[0])
 
     f32 = lambda v: v.astype(jnp.float32)
     m2, m1, m0 = f32(s2) - 0.5, f32(s1) - 0.5, f32(s0) - 0.5
@@ -393,12 +394,12 @@
             return jnp.where(s0 == 0, mine_d, other_d)
         return mine_d
 
-    def arrived(p, which, gap):
+    def arrived(p, which):
         last = lanes[which, 1]
         lower = sub < 4
 
         def load(c, t):
-            v = recv[pl.ds(c * SLOT + gap + p * NODES + t, 8, stride=2 * SLOT), :]
+            v = recv[pl.ds(c * SLOT + p * STRIDE + t, 8, stride=2 * SLOT), :]
             turned = pltpu.roll(v, 4, 0)
             u0, u1 = jnp.where(lower, v, turned), jnp.where(lower, turned, v)
             return jnp.where(last == 0, u0, pltpu.roll(u1, 64, 1)), jnp.where(last == 0, pltpu.roll(u0, 64, 1), u1)
@@ -472,7 +473,7 @@
                 told(3 + q)
                 tell(4 + q, steps_far[1 + q])
 
-        split(0, p, 2, arrived(p, 2, 0), twice(st0), wide=True)
+        split(0, p, 2, arrived(p, 2), twice(st0), wide=True)
 
         @pl.loop(0, 2)
         def _(which):
@@ -492,6 +493,8 @@
     )
     gift_out[0], gift_out[1] = fold(1, other_d)
     gift.start()
+    told(5)
+    tell(6, steps_far[3])
 
     @pl.loop(WIDE, PHASES)
     def _(p):
@@ -500,17 +503,15 @@
             @pl.when(p == q)
             def _():
                 await_piece(q)
-                told(3 + q)
-                if q == WIDE:
-                    tell(4 + q, steps_far[1 + q])
 
         def held(c, t):
             return tuple(st0[q * NODES + t, pl.ds(c, 8, stride=2), :] for q in range(2))
 
-        split(0, p, 0, arrived(p, 0, GAP), twice(st0))
+        split(0, p, 0, arrived(p, 0), twice(st0))
         split(1, p, 0, held, twice(st1))
         rest(p, 0)
 
+    told(6)
     gift.wait()
     totals = fold(0, mine_d)
     for h in range(2):
@@ -548,6 +549,13 @@
     for p in range(PHASES):
         for k in orders[p]:
             exchange(p, k).wait_send()
+
+    for e in range(16):
+        for half in range(2):
+
+            @pl.when(jnp.logical_not(mine(e, half)))
+            def _():
+                hand(e, half).wait_send()
 
     @pl.loop(0, 32)
     def _(g):
@@ -577,13 +585,6 @@
     )
     o_ref[0, 0] = picked[:4, :EV]
     o_ref[1, 0] = picked[:4, EV : 2 * EV]
-
-    for e in range(16):
-        for half in range(2):
-
-            @pl.when(jnp.logical_not(mine(e, half)))
-            def _():
-                hand(e, half).wait_send()
 
 
 def local(weights):
@@ -620,7 +621,7 @@
             dma((32,)),
         ],
         compiler_params=pltpu.CompilerParams(
-            collective_id=0, has_side_effects=True, vmem_limit_bytes=60 * 1024 * 1024
+            collective_id=0, has_side_effects=True, vmem_limit_bytes=54784 * 1024
         ),
     )(weights.reshape(ROWS, 4, 8, 128))
     return jnp.transpose(out, (3, 0, 1, 2))

time: 46.2 us -> 44.8 us (0.970)
  Pallas kernels: 44.8 us -> 44 us
  local copies, waits for them, and re-layouts: 1.28 us -> 0.6 us
    pallas_call x1, Pallas kernels: 44.8 us -> 44 us  [local(): pl.pallas_call(kernel, out_shape=jax.ShapeDtypeStruct((2, 1, 4, EV), jnp....]
    unnamed x1, local copies, waits for them, and re-layouts: 1.28 us -> 0.6 us
where the time goes in v3:
time: 44.8 us; the launch traced here: 44.7 us
  Pallas kernels  44 us (98%)
  local copies, waits for them, and re-layouts  0.6 us (1%)
    pallas_call x1, Pallas kernels, local(): pl.pallas_call(kernel, out_shape=jax.ShapeDtypeStruct((2, 1, 4, EV), jnp....  44 us

profile of v3, /device:TPU:1, one launch (start us, length us, event | category | flops | bytes accessed | tf_op | source)
XLA Modules:
  0.0 44.7 jit_solution(1617836751613971492)
XLA Ops:
  0.0 44.0 %shard_map.17 = f32[2,1,4,8]{3,2,1,0:T(4,128)S(1)} custom-call(f32[50,4,8,128]{3,2,1,0:T(8,128)} %bitcast.3), custom_call_target="tpu_custom_call" | custom-call | tf_op jit(solution)/shard_map/pallas_call | solution.py:593
  44.1 0.6 %copy.3 = f32[8,2,1,4]{0,3,2,1:T(4,128)} copy(f32[8,2,1,4]{0,3,2,1:T(4,128)S(1)} %bitcast.2) | data formatting | bytes 512

commit v4 on v3

--- a/solution.py
+++ b/solution.py
@@ -245,8 +245,7 @@
     for p in range(WIDE, PHASES):
         pack(p)
     told(2)
-    for p in range(WIDE, PHASES):
-        ship(p)
+    ship(WIDE)
     tell(3, steps_far[0])
 
     f32 = lambda v: v.astype(jnp.float32)
@@ -474,6 +473,11 @@
                 tell(4 + q, steps_far[1 + q])
 
         split(0, p, 2, arrived(p, 2), twice(st0), wide=True)
+
+        @pl.when(p == 0)
+        def _():
+            for q in range(WIDE + 1, PHASES):
+                ship(q)
 
         @pl.loop(0, 2)
         def _(which):

time: 44.8 us -> 44.8 us (level)
  no operation moved by 1% of the time
where the time goes in v4:
time: 44.8 us; the launch traced here: 44.6 us
  Pallas kernels  44 us (98%)
  local copies, waits for them, and re-layouts  0.6 us (1%)
    pallas_call x1, Pallas kernels, local(): pl.pallas_call(kernel, out_shape=jax.ShapeDtypeStruct((2, 1, 4, EV), jnp....  44 us

profile of v4, /device:TPU:1, one launch (start us, length us, event | category | flops | bytes accessed | tf_op | source)
XLA Modules:
  0.0 44.6 jit_solution(13006253012615902479)
XLA Ops:
  0.0 44.0 %shard_map.17 = f32[2,1,4,8]{3,2,1,0:T(4,128)S(1)} custom-call(f32[50,4,8,128]{3,2,1,0:T(8,128)} %bitcast.3), custom_call_target="tpu_custom_call" | custom-call | tf_op jit(solution)/shard_map/pallas_call | solution.py:597
  44.0 0.6 %copy.3 = f32[8,2,1,4]{0,3,2,1:T(4,128)} copy(f32[8,2,1,4]{0,3,2,1:T(4,128)S(1)} %bitcast.2) | data formatting | bytes 512
